TPU v7x, 32 devices: a whole 2x2x4 slice. The times are simulated.
32 devices in a mesh: grp: 2 (over y), node: 4 (over z), sub: 2 (over x), rep: 2 (over core).
Axes of the slice: x: 2, y: 2, z: 4, core: 2. Of those that a mesh axis runs over, the one named last changes fastest.
Arguments:
- meson_nodes: float32 [2, 16, 512, 512], P(None, ('grp', 'node'), 'sub', 'rep'), parts along dimension 1, may hold values from -0.66 to 0.66
- term_nodes: int32 [8, 2], P('grp'), parts along dimension 0, may hold values from 0 to 7, as said below
- weight_codes: int32 [8], P('grp'), parts along dimension 0, may hold values from 0 to 7
- resident_pick: int32 [16], P('grp'), parts along dimension 0, may hold values from 0 to 1
Outputs:
- contracted: float32 [2, 16, 512, 512], P(None, ('grp', 'node'), 'sub', 'rep'), parts along dimension 1
There are 2 independent parts, one for each index of `grp`. A program takes and returns all parts, laid end to end along the dimension named above; each array names one. Nothing has to cross between parts.
Inputs may be any that keep to these rules, and one draw needn't show every extreme that they name: `term_nodes`: node n belongs to owner n // 2. In every term the two nodes differ. The first nodes of at most 2 terms belong to any one owner, and those of exactly 2 terms to some owner.
All inputs are finite; a program needn't handle non-finite values.
Results may differ from a plain program's by a relative error of at most 0.000098.
Values sent between devices are 32-bit elements; how exact they have to be, the bound alone decides.
No kernel may reach another device: no remote copies, remote signals or barrier semaphores. Data moves between devices by JAX's collectives and lax.ppermute only.
A program may use at most 64 MiB of HBM per device.

v0:
```python
import functools

import jax
import jax.numpy as jnp
from jax import lax
from jax.experimental import pallas as pl
from jax.experimental.pallas import tpu as pltpu
from jax.sharding import PartitionSpec as P

VMEM_BYTES = 20 * 2**20
UNROLLED = 3
FIRST_OVER = 2


def round_bound(line, owned, terms):
    most = min(terms, owned)
    for hop in range(2, line):
        most = max(min(terms, owned * hop), most + 1)
    return max(most, FIRST_OVER) + terms


def plan_kernel(line, owned, terms, rounds, opened, *refs):
    place_ref, all_terms_ref, codes_ref, slot_ref, weight_ref, table_ref, length_ref, terms_ref, sem = refs
    fetch(all_terms_ref, terms_ref, sem)
    count = line * owned
    shape = (line, count)
    ids = lax.broadcasted_iota(jnp.int32, shape, 1)
    place = lax.broadcasted_iota(jnp.int32, shape, 0)
    home = ids // owned
    lowest, highest = home, home
    wanted = jnp.zeros(shape, jnp.float32)
    me = place_ref[0]
    even = lax.rem(me, 2) == 0
    pairs = [(terms_ref[0, t], terms_ref[1, t]) for t in range(terms)]
    for a, b in pairs:
        first_home, second_home = a // owned, b // owned
        other = jnp.where(ids == a, second_home, jnp.where(ids == b, first_home, home))
        lowest = jnp.minimum(lowest, other)
        highest = jnp.maximum(highest, other)
        wanted = jnp.where((place == first_home) & (ids == b) & (home != place), 1.0, wanted)

    def pick(score):
        best = jnp.max(score, axis=1, keepdims=True)
        chosen = jnp.where((score == best) & (score > 0.0), 1.0, 0.0)
        return best, chosen, jnp.sum(chosen * (ids - count).astype(jnp.float32), axis=1, keepdims=True) + float(count)

    def anywhere(chosen):
        return jnp.max(chosen, axis=0, keepdims=True).astype(jnp.int32)

    rank = lax.broadcasted_iota(jnp.int32, (line, 1), 0)

    def of(send, who):
        return jnp.sum(jnp.where(rank == who, send - float(count), 0.0), axis=0, keepdims=True).astype(jnp.int32) + count

    names = [jnp.full((1, 1), me * owned + m, jnp.int32) for m in range(owned)]

    def write(row, send):
        wanted_name = of(send, me)
        slot = jnp.zeros((1, 1), jnp.float32)
        for k, name in enumerate(names):
            slot = jnp.where(wanted_name == name, float(k), slot)
        slot_ref[row] = jnp.broadcast_to(slot, slot_ref.shape[1:])
        return wanted_name

    left, right = home, home
    lane = lax.broadcasted_iota(jnp.int32, (line, 2), 1)
    length = jnp.zeros((line, 2), jnp.int32)
    gone = []
    for step in range(rounds):
        to_go = jnp.where((left == place) & (lowest < place), place - lowest, 0)
        best_left, moved_left, send_left = pick(jnp.where(to_go > 0, (to_go + 1) * count - ids, 0).astype(jnp.float32))
        to_go = jnp.where((right == place) & (highest > place), highest - place, 0)
        best_right, moved_right, send_right = pick(jnp.where(to_go > 0, (to_go + 1) * count - ids, 0).astype(jnp.float32))
        busy_line = jnp.max(jnp.maximum(best_left, best_right), axis=0, keepdims=True)
        if step >= FIRST_OVER:
            here = ((left <= place) & (place < home)) | ((right >= place) & (place > home))
            best_over, moved_over, send_over = pick(jnp.where(here, wanted * (count - ids).astype(jnp.float32), 0.0))
            wanted = wanted - moved_over
            busy = jnp.maximum(busy_line, jnp.max(best_over, axis=0, keepdims=True))
        else:
            send_over, busy = jnp.full((line, 1), float(count), jnp.float32), busy_line
        for i, send in enumerate((send_left, send_right, send_over)):
            table_ref[3 * step + i] = send.astype(jnp.int32)
        if step <= opened:
            first = jnp.where(even, send_right, send_left)
            second = jnp.where(even, send_left, send_right)
            for i, send in enumerate((first, second, send_over)):
                name = write(3 * step + i, send)
                if i == 2 and step >= FIRST_OVER:
                    gone.append(name)
            come_left, come_right = of(send_left, me + 1), of(send_right, me - 1)
            names += [jnp.where(even, come_left, come_right), jnp.where(even, come_right, come_left)]
        left = left - anywhere(moved_left)
        right = right + anywhere(moved_right)
        length = jnp.where(jnp.where(lane == 0, busy_line, busy) > 0.0, step + 1, length)
    length_ref[0] = jnp.max(length[:, :1].astype(jnp.float32)).astype(jnp.int32)
    length_ref[1] = jnp.max(length[:, 1:].astype(jnp.float32)).astype(jnp.int32)

    names = names[: owned + 2 * opened]
    row = 0
    for side, queue in ((0, names), (1, names), (0, gone)):
        for n in range(owned):
            scales = [
                jnp.where(ours[side] == me * owned + n, (codes_ref[t].astype(jnp.float32) - 3.5) * 0.5, 0.0)
                for t, ours in enumerate(pairs)
            ]
            for name in queue:
                weight = jnp.zeros((1, 1), jnp.float32)
                for scale, ours in zip(scales, pairs):
                    weight = weight + jnp.where(name == ours[1 - side], scale, 0.0)
                weight_ref[row] = jnp.broadcast_to(weight, weight_ref.shape[1:])
                row += 1


def plan_rounds(me, term_nodes, weight_codes, line, owned, rounds, opened, cols):
    overs = opened + 1 - FIRST_OVER
    rows = owned * (2 * (owned + 2 * opened) + overs)
    slots, weights, tables, lengths = pl.pallas_call(
        functools.partial(plan_kernel, line, owned, term_nodes.shape[1], rounds, opened),
        out_shape=[
            jax.ShapeDtypeStruct((3 * (opened + 1), 1, 128), jnp.float32),
            jax.ShapeDtypeStruct((rows, 1, cols), jnp.float32),
            jax.ShapeDtypeStruct((3 * rounds, line, 1), jnp.int32),
            jax.ShapeDtypeStruct((2,), jnp.int32),
        ],
        in_specs=[pl.BlockSpec(memory_space=space) for space in (pltpu.SMEM, pl.ANY, pltpu.SMEM)],
        scratch_shapes=[pltpu.SMEM(term_nodes.shape, jnp.int32), pltpu.SemaphoreType.DMA],
        out_specs=[pl.BlockSpec(memory_space=pltpu.VMEM)] * 3 + [pl.BlockSpec(memory_space=pltpu.SMEM)],
        cost_estimate=pl.CostEstimate(flops=1000, bytes_accessed=1000, transcendentals=0),
    )(me, term_nodes, weight_codes)
    return slots, weights, tables, lengths


def split(value):
    high = value.astype(jnp.bfloat16)
    return high, (value - high.astype(jnp.float32)).astype(jnp.bfloat16)


def product(left, right_real, right_imag):
    rows = left.shape[2]
    every = left.reshape(4 * rows, left.shape[3])
    dot = functools.partial(jnp.dot, preferred_element_type=jnp.float32)

    def times(high, low):
        one, two = dot(every, high), dot(every[: 2 * rows], low)
        both = one[: 2 * rows] + (one[2 * rows :] + two)
        return both[:rows], both[rows:]

    real_real, imag_real = times(*right_real)
    real_imag, imag_imag = times(*right_imag)
    return real_real - imag_imag, real_imag + imag_real


def put_left(ref, n, c, cols, value):
    for part, piece in enumerate(split(value)):
        ref[n, part, c, :, cols] = piece


def put_right(ref, n, c, rows, value):
    for part, piece in enumerate(split(value)):
        ref[n, c, part, rows, :] = piece


def right_parts(ref, n):
    return [(ref[n, c, 0], ref[n, c, 1]) for c in range(2)]


def block(index, size):
    return pl.ds(pl.multiple_of(index * size, size), size)


def fetch(terms_ref, terms_here, sem):
    copy = pltpu.make_async_copy(terms_ref, terms_here, sem)
    copy.start()
    copy.wait()


def copy_chosen(slots, nodes, outs, sems):
    for i, (slot, out_ref) in enumerate(zip(slots, outs)):
        for k, node in enumerate(nodes):

            @pl.when(slot == k)
            def _(node=node, out_ref=out_ref, i=i):
                pltpu.make_async_copy(node, out_ref, sems.at[i]).start()

    return [pltpu.make_async_copy(nodes[0], out_ref, sems.at[i]) for i, out_ref in enumerate(outs)]


def first_kernel(line, owned, terms, place_ref, terms_ref, own_ref, first_ref, second_ref, *refs):
    copies, (terms_here, sem, sems) = refs[:owned], refs[owned:]
    moves = [
        pltpu.make_async_copy(own_ref.at[c, m], copies[m].at[c], sems.at[c, m]) for m in range(owned) for c in range(2)
    ]
    fetch = pltpu.make_async_copy(terms_ref, terms_here, sem)
    for move in [fetch, *moves]:
        move.start()
    fetch.wait()
    me = place_ref[0]
    choice = []
    lows, highs = [jnp.int32(0)] * owned, [jnp.int32(0)] * owned
    for t in range(terms):
        a, b = terms_here[0, t], terms_here[1, t]
        to_second, to_first = b // owned - me, a // owned - me
        for m in range(owned):
            name = me * owned + m
            away = jnp.where(a == name, to_second, jnp.where(b == name, to_first, 0))
            lows[m] = jnp.maximum(lows[m], -away)
            highs[m] = jnp.maximum(highs[m], away)
    for far in (lows, highs):
        best, slot = far[0], jnp.int32(0)
        for m in range(1, owned):
            slot = jnp.where(far[m] > best, m, slot)
            best = jnp.maximum(far[m], best)
        choice.append(slot)
    even = lax.rem(me, 2) == 0
    slots = (jnp.where(even, choice[1], choice[0]), jnp.where(even, choice[0], choice[1]))
    for move in moves:
        move.wait()
    for slot, out_ref in zip(slots, (first_ref, second_ref)):
        for m in range(owned):

            @pl.when(slot == m)
            def _(m=m, out_ref=out_ref):
                out_ref[...] = copies[m][...]


def choose_kernel(rows, slot_ref, *refs):
    count = len(refs) - 1 - len(rows)
    slots = [jnp.max(slot_ref[row]).astype(jnp.int32) for row in rows]
    for copy in copy_chosen(slots, refs[:count], refs[count:-1], refs[-1]):
        copy.wait()


def early_kernel(subs, reps, names, place_ref, weight_ref, *refs):
    outs = 2 + subs - 1 + 2
    refs, (u_ref, v_ref, *rest) = refs[: len(refs) - outs], refs[len(refs) - outs :]
    x_refs, (row_ref, col_ref) = rest[: subs - 1], rest[subs - 1 :]
    own, beside, refs = refs[0], refs[1:reps], refs[reps:]
    rows, cols = own.shape[2:]
    owned = own.shape[1]
    across = [refs[m * (subs - 1) : (m + 1) * (subs - 1)] for m in range(owned)]
    arrived = refs[owned * (subs - 1) :]
    for n in range(owned):
        for c in range(2):
            for i in range(reps):
                at = block(place_ref[1 + subs + i], cols)
                put_left(row_ref, n, c, at, (own if i == 0 else beside[i - 1])[c, n])
            for i in range(subs):
                matrix = own[c, n] if i == 0 else across[n][i - 1][c]
                put_right(col_ref, n, c, block(place_ref[1 + i], rows), matrix)
            nodes = [own[c, m] for m in range(owned)] + [a[c] for a in arrived]
            u_ref[n, c] = sum(weight_ref[n * names + k] * node for k, node in enumerate(nodes))
            v_ref[n, c] = sum(weight_ref[(owned + n) * names + k] * node for k, node in enumerate(nodes))
            for j in range(subs - 1):
                x_refs[j][n, c] = sum(weight_ref[n * names + m] * across[m][j][c] for m in range(owned))


def sum_kernel(subs, reps, names, gone, seen, arrived, place_ref, weight_ref, row_ref, col_ref, *refs):
    u, v, refs = refs[:subs], refs[subs : subs + reps], refs[subs + reps :]
    came = [refs[i * arrived : (i + 1) * arrived] for i in range(reps)]
    items, over, (out_ref, left_ref, v_parts, u_parts) = came[0], refs[reps * arrived : -4], refs[-4:]
    rows, cols = out_ref.shape[2:]
    owned = out_ref.shape[0]
    for n in range(owned):
        for c in range(2):
            for i in range(subs):
                total = u[i][n, c]
                if i == 0:
                    for k, item in enumerate(items):
                        total = total + weight_ref[n * names + seen + k] * item[c]
                else:
                    for k, item in enumerate(over[i - 1 :: subs - 1]):
                        total = total + weight_ref[2 * owned * names + n * gone + k] * item[c]
                put_right(u_parts, n, c, block(place_ref[1 + i], rows), total)
            for i in range(reps):
                total = v[i][n, c]
                for k, item in enumerate(came[i]):
                    total = total + weight_ref[(owned + n) * names + seen + k] * item[c]
                put_left(v_parts, n, c, block(place_ref[1 + subs + i], cols), total)
        one = product(row_ref[n], *right_parts(u_parts, n))
        two = product(v_parts[n], *right_parts(col_ref, n))
        out_ref[n, 0] = one[0] + two[0]
        out_ref[n, 1] = one[1] + two[1]
        for j in range(subs - 1):
            left_ref[j, n] = row_ref[n, :, :, :, block(place_ref[2 + j], rows)]


def late_kernel(subs, first, stride, weight_ref, sum_ref, left_ref, *refs):
    over, out_ref = refs[: subs - 1], refs[subs - 1]
    for n in range(sum_ref.shape[0]):
        real, imag = sum_ref[n, 0], sum_ref[n, 1]
        for j in range(subs - 1):
            one = product(left_ref[j, n], *[split(weight_ref[first + stride * n] * over[j][c]) for c in range(2)])
            real, imag = real + one[0], imag + one[1]
        out_ref[n, 0] = real
        out_ref[n, 1] = imag


def times_resident(cells, i, place_ref, pick_ref, col_ref, s_ref, n):
    at = block(place_ref[1 + cells + i], s_ref.shape[3])
    node = pick_ref[place_ref[0] * s_ref.shape[0] + n]
    parts = [split(s_ref[n, c]) for c in range(2)]
    left = jnp.stack([jnp.stack([parts[c][part] for c in range(2)]) for part in range(2)])
    return product(left, *[(col_ref[node, c, 0, at, :], col_ref[node, c, 1, at, :]) for c in range(2)])


def half_kernel(cells, place_ref, pick_ref, col_ref, s_ref, out_ref):
    for n in range(s_ref.shape[0]):
        out_ref[0, n], out_ref[1, n] = times_resident(cells, 0, place_ref, pick_ref, col_ref, s_ref, n)


def last_kernel(cells, place_ref, pick_ref, col_ref, half_ref, *refs):
    for n in range(half_ref.shape[1]):
        real, imag = half_ref[0, n], half_ref[1, n]
        for i, s_ref in enumerate(refs[:-1]):
            one = times_resident(cells, 1 + i, place_ref, pick_ref, col_ref, s_ref, n)
            real, imag = real + one[0], imag + one[1]
        refs[-1][0, n] = real
        refs[-1][1, n] = imag


def way_kernel(groups, fixed, *refs):
    lengths, out_ref = refs[:groups], refs[groups]
    way = jnp.int32(0)
    for length in lengths:
        way = jnp.maximum(way, jnp.maximum(length[0] - fixed, length[1] - fixed - 1))
    out_ref[0] = jnp.minimum(way, 2)


def call(kernel, scalars, arrays, outs, scratch=()):
    return pl.pallas_call(
        kernel,
        out_shape=outs,
        in_specs=[pl.BlockSpec(memory_space=pltpu.SMEM)] * len(scalars)
        + [pl.BlockSpec(memory_space=pltpu.VMEM)] * len(arrays),
        out_specs=jax.tree.map(lambda _: pl.BlockSpec(memory_space=pltpu.VMEM), outs),
        scratch_shapes=list(scratch),
        compiler_params=pltpu.CompilerParams(vmem_limit_bytes=VMEM_BYTES),
        cost_estimate=pl.CostEstimate(flops=1000, bytes_accessed=1000, transcendentals=0),
    )(*scalars, *arrays)


def shifts(array, axis):
    size = lax.axis_size(axis)
    return [lax.ppermute(array, axis, [(i, (i + j) % size) for i in range(size)]) for j in range(1, size)]


def places(axis):
    size = lax.axis_size(axis)
    return [(lax.axis_index(axis) - j) % size for j in range(size)]


def body(meson_nodes, term_nodes, weight_codes, resident_pick):
    line = lax.axis_size("node")
    subs, reps = lax.axis_size("sub"), lax.axis_size("rep")
    _, owned, rows, cols = meson_nodes.shape
    count = owned * line
    terms = term_nodes.shape[0]
    me = lax.axis_index("node")
    base = me * owned
    to_left = [(z + 1, z) for z in range(line - 1)]
    to_right = [(z, z + 1) for z in range(line - 1)]
    node_shape = (2, rows, cols)
    nodes_shape = (owned, 2, rows, cols)
    depth = rows * subs
    fixed = min(line - 1, UNROLLED)
    opened = fixed + 1

    def out(shape, dtype=jnp.float32):
        return jax.ShapeDtypeStruct(shape, dtype)

    def near(shape, dtype=jnp.float32):
        return pltpu.VMEM(shape, dtype)

    place = jnp.stack([me, *places("sub"), *places("rep")]).astype(jnp.int32)
    slots, weights, tables, length = plan_rounds(
        place, term_nodes.T, weight_codes, line, owned, round_bound(line, owned, terms), opened, cols
    )

    names = owned + 2 * opened
    gone = opened + 1 - FIRST_OVER
    pairs = [[(z, z + 1) for z in range(start, line - 1, 2)] for start in range(2)]
    swaps = [pair + [(j, i) for i, j in pair] for pair in pairs]

    def choose(step, kinds, came):
        nodes = [*own, *came]
        return pl.pallas_call(
            functools.partial(choose_kernel, [3 * step + kind for kind in kinds]),
            out_shape=[out(node_shape)] * len(kinds),
            in_specs=[pl.BlockSpec(memory_space=pltpu.VMEM)] + [pl.BlockSpec(memory_space=pl.ANY)] * len(nodes),
            out_specs=[pl.BlockSpec(memory_space=pltpu.VMEM)] * len(kinds),
            scratch_shapes=[pltpu.SemaphoreType.DMA((len(kinds),))],
            compiler_params=pltpu.CompilerParams(vmem_limit_bytes=VMEM_BYTES),
            cost_estimate=pl.CostEstimate(flops=1000, bytes_accessed=1000, transcendentals=0),
        )(slots, *nodes)

    def meet(first, second):
        return [lax.ppermute(item, "node", swap) for item, swap in zip((first, second), swaps)]

    first, second, *own = pl.pallas_call(
        functools.partial(first_kernel, line, owned, terms),
        out_shape=[out(node_shape)] * (2 + owned),
        in_specs=[pl.BlockSpec(memory_space=space) for space in (pltpu.SMEM, pl.ANY, pl.ANY)],
        out_specs=[pl.BlockSpec(memory_space=pltpu.VMEM)] * (2 + owned),
        scratch_shapes=[
            pltpu.SMEM(term_nodes.shape[::-1], jnp.int32),
            pltpu.SemaphoreType.DMA,
            pltpu.SemaphoreType.DMA((2, owned)),
        ],
        compiler_params=pltpu.CompilerParams(vmem_limit_bytes=VMEM_BYTES),
        cost_estimate=pl.CostEstimate(flops=1000, bytes_accessed=1000, transcendentals=0),
    )(place, term_nodes.T, meson_nodes)
    came, across, over = [], [], []
    lengths = [length, *shifts(length, "grp")]
    for step in range(fixed):
        if step < FIRST_OVER:
            beyond = own[step : owned if step == FIRST_OVER - 1 else step + 1]
            if step > 0:
                first, second = choose(step, (0, 1), came)
        else:
            first, second, *beyond = choose(step, (0, 1, 2), came)
        beyond = [x for item in beyond for x in shifts(item, "sub")]
        new, beyond = lax.optimization_barrier((meet(first, second), beyond))
        came = came + new
        if step < FIRST_OVER:
            across = across + beyond
        else:
            over = over + beyond
        if step == FIRST_OVER - 1:
            beside = shifts(meson_nodes, "rep")
            came, beside, lengths = lax.optimization_barrier((came, beside, lengths))
            before = len(came)
            way = pl.pallas_call(
                functools.partial(way_kernel, len(lengths), fixed),
                out_shape=jax.ShapeDtypeStruct((1,), jnp.int32),
                in_specs=[pl.BlockSpec(memory_space=pltpu.SMEM)] * len(lengths),
                out_specs=pl.BlockSpec(memory_space=pltpu.SMEM),
            )(*lengths)

    row_part, col_part = (owned, 2, 2, rows, depth), (owned, 2, 2, depth, cols)

    def begin(beside, across, came):
        *mixed, row, col = call(
            functools.partial(early_kernel, subs, reps, names),
            [place],
            [weights, meson_nodes, *beside, *across, *came],
            [out(nodes_shape), near(nodes_shape)]
            + [out(nodes_shape)] * (subs - 1)
            + [out(row_part, jnp.bfloat16), out(col_part, jnp.bfloat16)],
        )
        return mixed, row, col

    early, row, col = begin(beside, across, came[:before])

    def sums(row, col, u, v, items=(), over=()):
        return call(
            functools.partial(sum_kernel, subs, reps, names, gone, owned + before, len(items) // reps),
            [place],
            [weights, row, col, *u, *v, *items, *over],
            [out(nodes_shape), out((subs - 1, owned, 2, 2, rows, rows), jnp.bfloat16)],
            [pltpu.VMEM(row_part, jnp.bfloat16), pltpu.VMEM(col_part, jnp.bfloat16)],
        )

    def beyond_rep(items):
        there = [shifts(item, "rep") for item in items]
        return [*items, *[each[j] for j in range(reps - 1) for each in there]]

    u, *ux = early[:1] + early[2:]

    def end(step, came, over):
        [item] = choose(step, (2,), came)
        late = shifts(item, "sub")
        fresh = beyond_rep(came[before:])
        v = [early[1], *shifts(early[1], "rep")]
        first = 2 * owned * names + step - FIRST_OVER
        return call(
            functools.partial(late_kernel, subs, first, gone),
            [],
            [weights, *sums(row, col, [u, *ux], v, fresh, over), *late],
            out(nodes_shape),
        )

    def short(_):
        return end(fixed, came, over)

    def middle(_):
        first, second, item = choose(fixed, (0, 1, 2), came)
        new, beyond = lax.optimization_barrier((meet(first, second), shifts(item, "sub")))
        return end(fixed + 1, came + new, over + beyond)

    def long(_):
        edges = jnp.pad(tables.reshape(-1, 3, line), ((0, 0), (0, 0), (1, 1)), constant_values=count)
        mine = lax.dynamic_slice_in_dim(edges, me, 3, axis=2)
        rounds = functools.reduce(jnp.maximum, [length[1] for length in lengths])
        leading, trailing = term_nodes[:, 0], term_nodes[:, 1]
        factors = (weight_codes.astype(jnp.float32) - 3.5) * 0.5
        mine_ids = base + jnp.arange(owned, dtype=jnp.int32)
        first_mine = factors[:, None] * (leading[:, None] == mine_ids)
        second_mine = factors[:, None] * (trailing[:, None] == mine_ids)
        held = jnp.zeros((count + 1, 2, rows, cols), jnp.float32)
        held = lax.dynamic_update_slice(held, jnp.swapaxes(meson_nodes, 0, 1), (base, 0, 0, 0))
        across = [x for m in range(owned) for x in shifts(meson_nodes[:, m], "sub")]
        (u, v, *ux), row, col = begin(shifts(meson_nodes, "rep"), across, [])

        def add(total, mine_terms, others, name, item):
            scale = jnp.sum(mine_terms * (others == name)[:, None], axis=0)
            return total + scale[:, None, None, None] * item[None]

        def more(state):
            return state[0] < rounds

        def again(state):
            step, held, u, v = state
            ids = lax.dynamic_index_in_dim(mine, step, 0, keepdims=False)
            left, right, item = lax.optimization_barrier(
                tuple(lax.dynamic_index_in_dim(held, ids[i, 1], 0, keepdims=False) for i in range(3))
            )
            from_right = lax.ppermute(left, "node", to_left)
            from_left = lax.ppermute(right, "node", to_right)
            items = [item, *shifts(item, "sub")]
            from_right, from_left = lax.optimization_barrier((from_right, from_left))
            u = [add(total, first_mine, trailing, ids[2, 1], x) for total, x in zip(u, items)]
            v = add(v, second_mine, leading, ids[0, 2], from_right)
            v = add(v, second_mine, leading, ids[1, 0], from_left)
            held = lax.dynamic_update_slice_in_dim(held, from_right[None], ids[0, 2], 0)
            held = lax.dynamic_update_slice_in_dim(held, from_left[None], ids[1, 0], 0)
            return step + 1, held, u, v

        _, _, u, v = lax.while_loop(more, again, (jnp.int32(0), held, [u, *ux], v))
        return sums(row, col, u, [v, *shifts(v, "rep")])[0]

    summed = lax.switch(way[0], [short, middle, long], None)
    half = call(functools.partial(half_kernel, subs), [place, resident_pick], [col, summed], out(meson_nodes.shape))
    return call(
        functools.partial(last_kernel, subs),
        [place, resident_pick],
        [col, half, *shifts(summed, "rep")],
        out(meson_nodes.shape),
    )


def solution(mesh):
    in_specs = (P(None, ("grp", "node"), "sub", "rep"), P("grp", None), P("grp"), P("grp"))
    out_specs = P(None, ("grp", "node"), "sub", "rep")
    return jax.shard_map(body, mesh=mesh, in_specs=in_specs, out_specs=out_specs, check_vma=False)
```

profile of v0, /device:TPU:0, one launch (start us, length us, event | category | flops | bytes accessed | tf_op | source)
XLA Modules:
  0.0 76.5 jit_solution(12106805885120382278)
XLA Ops:
  0.1 2.8 %shard_map.47 = (f32[2,256,256]{2,1,0:T(8,128)S(1)}, f32[2,256,256]{2,1,0:T(8,128)S(1)}, f32[2,256,256]{2,1,0:T(8,128)}, f32[2,256,256]{2,1,0:T(8,128)}) custom-call(s32[5]{0:T(128)S(1)} %stack.23.refs_0_.place_ref, s32[2,4]{1,0:T(2,128)} %bitcast.55, f32[2,2,256,256]{3,2,1,0:T(8,128)} %refs_0_.1), custom_call_target="tpu_custom_call" | custom-call | flops 1000 | bytes 1000 | tf_op jit(solution)/shard_map/pallas_call | solution.py:400
  2.9 3.1 %collective-permute-start.20 = (f32[2,256,256]{2,1,0:T(8,128)S(1)}, f32[2,256,256]{2,1,0:T(8,128)}, u32[]{:S(2)}, u32[]{:S(2)}) collective-permute-start(f32[2,256,256]{2,1,0:T(8,128)S(1)} %get-tuple-element.257), channel_id=1, source_target_pairs={{0,4},{8,12},{4,0},{12,8},{1,5},{9,13},{5,1},{13,9},{2,6},{10,14},... | collective-permute-start | bytes 1572872 | tf_op jit(solution)/shard_map/ppermute | solution.py:398
  6.0 1.5 %collective-permute-start.21 = (f32[2,256,256]{2,1,0:T(8,128)S(1)}, f32[2,256,256]{2,1,0:T(8,128)}, u32[]{:S(2)}, u32[]{:S(2)}) collective-permute-start(f32[2,256,256]{2,1,0:T(8,128)S(1)} %get-tuple-element.258), channel_id=1, source_target_pairs={{4,8},{8,4},{5,9},{9,5},{6,10},{10,6},{7,11},{11,7},{20,24},{24,20... | collective-permute-start | bytes 1572872 | tf_op jit(solution)/shard_map/ppermute | solution.py:398
  7.5 1.5 %collective-permute-start.22 = (f32[2,256,256]{2,1,0:T(8,128)}, f32[2,256,256]{2,1,0:T(8,128)S(1)}, u32[]{:S(2)}, u32[]{:S(2)}) collective-permute-start(f32[2,256,256]{2,1,0:T(8,128)} %get-tuple-element.259.refs_0_), channel_id=1, source_target_pairs={{0,2},{2,0},{1,3},{3,1},{4,6},{6,4},{5,7},{7,5},{8,10},{10,8},{9,1... | collective-permute-start | bytes 1572872 | tf_op jit(solution)/shard_map/ppermute | solution.py:345
  9.5 3.0 %shard_map.46 = (f32[15,1,128]{2,1,0:T(1,128)S(1)}, f32[46,1,256]{2,1,0:T(1,128)S(1)}, s32[27,4,1]{2,1,0:T(4,128)S(1)}, s32[2]{0:T(128)S(1)}) custom-call(s32[5]{0:T(128)S(1)} %stack.23.refs_0_.place_ref, s32[2,4]{1,0:T(2,128)} %bitcast.56, s32[4]{0:T(128)} %refs_2_.1), custom_call_target="tpu_custom_call" | custom-call | flops 1000 | bytes 1000 | tf_op jit(solution)/shard_map/pallas_call | solution.py:118
  12.5 5.5 %collective-permute-done.20.refs_2_.refs_4_ = f32[2,256,256]{2,1,0:T(8,128)} collective-permute-done((f32[2,256,256]{2,1,0:T(8,128)S(1)}, f32[2,256,256]{2,1,0:T(8,128)}, u32[]{:S(2)}, u32[]{:S(2)}) %collective-permute-start.20) | collective-permute-done | bytes 524320 | tf_op jit(solution)/shard_map/ppermute | solution.py:398
  18.0 4.5 %collective-permute-done.22.refs_2_ = f32[2,256,256]{2,1,0:T(8,128)S(1)} collective-permute-done((f32[2,256,256]{2,1,0:T(8,128)}, f32[2,256,256]{2,1,0:T(8,128)S(1)}, u32[]{:S(2)}, u32[]{:S(2)}) %collective-permute-start.22) | collective-permute-done | bytes 524320 | tf_op jit(solution)/shard_map/ppermute | solution.py:345
  23.9 3.8 %collective-permute-start.23 = (f32[2,256,256]{2,1,0:T(8,128)S(1)}, f32[2,256,256]{2,1,0:T(8,128)S(1)}, u32[]{:S(2)}, u32[]{:S(2)}) collective-permute-start(f32[2,256,256]{2,1,0:T(8,128)S(1)} %get-tuple-element.264), channel_id=1, source_target_pairs={{0,4},{8,12},{4,0},{12,8},{1,5},{9,13},{5,1},{13,9},{2,6},{10,14},... | collective-permute-start | bytes 1572872 | tf_op jit(solution)/shard_map/ppermute | solution.py:398
  28.4 1.5 %collective-permute-start.27 = (s32[2]{0:T(128)S(1)}, s32[2]{0:T(128)S(1)}, u32[]{:S(2)}, u32[]{:S(2)}) collective-permute-start(s32[2]{0:T(128)S(1)} %get-tuple-element.277.refs_0_), channel_id=1, source_target_pairs={{0,16},{16,0},{1,17},{17,1},{2,18},{18,2},{3,19},{19,3},{4,20},{20... | collective-permute-start | bytes 32 | tf_op jit(solution)/shard_map/ppermute | solution.py:345
  29.9 2.4 %collective-permute-done.25.refs_3_ = f32[2,256,256]{2,1,0:T(8,128)S(1)} collective-permute-done((f32[2,256,256]{2,1,0:T(8,128)}, f32[2,256,256]{2,1,0:T(8,128)S(1)}, u32[]{:S(2)}, u32[]{:S(2)}) %collective-permute-start.25) | collective-permute-done | bytes 524320 | tf_op jit(solution)/shard_map/ppermute | solution.py:345
  32.3 4.2 %collective-permute-done.23.refs_6_.refs_4_ = f32[2,256,256]{2,1,0:T(8,128)S(1)} collective-permute-done((f32[2,256,256]{2,1,0:T(8,128)S(1)}, f32[2,256,256]{2,1,0:T(8,128)S(1)}, u32[]{:S(2)}, u32[]{:S(2)}) %collective-permute-start.23) | collective-permute-done | bytes 524320 | tf_op jit(solution)/shard_map/ppermute | solution.py:398
  36.5 2.6 %shard_map.51 = (f32[2,256,256]{2,1,0:T(8,128)}, f32[2,256,256]{2,1,0:T(8,128)}, f32[2,256,256]{2,1,0:T(8,128)}) custom-call(f32[15,1,128]{2,1,0:T(1,128)S(1)} %get-tuple-element.262.slot_ref, f32[2,256,256]{2,1,0:T(8,128)} %get-tuple-element.259.refs_0_, f32[2,256,256]{2,1,0:T(8,128)} %get-tuple-element.263.refs_1_, ...), custom_call_target="tpu_custom_call" | custom-call | flops 1000 | bytes 1000 | tf_op jit(solution)/shard_map/pallas_call | solution.py:387
  39.1 2.6 %collective-permute-start.28 = (f32[2,256,256]{2,1,0:T(8,128)}, f32[2,256,256]{2,1,0:T(8,128)}, u32[]{:S(2)}, u32[]{:S(2)}) collective-permute-start(f32[2,256,256]{2,1,0:T(8,128)} %get-tuple-element.280), channel_id=1, source_target_pairs={{0,4},{8,12},{4,0},{12,8},{1,5},{9,13},{5,1},{13,9},{2,6},{10,14},... | collective-permute-start | bytes 1572872 | tf_op jit(solution)/shard_map/ppermute | solution.py:398
  43.1 1.5 %collective-permute-start.30 = (f32[2,256,256]{2,1,0:T(8,128)}, f32[2,256,256]{2,1,0:T(8,128)}, u32[]{:S(2)}, u32[]{:S(2)}) collective-permute-start(f32[2,256,256]{2,1,0:T(8,128)} %get-tuple-element.282), channel_id=1, source_target_pairs={{0,2},{2,0},{1,3},{3,1},{4,6},{6,4},{5,7},{7,5},{8,10},{10,8},{9,1... | collective-permute-start | bytes 1572872 | tf_op jit(solution)/shard_map/ppermute | solution.py:345
  44.6 4.6 %shard_map.49 = (f32[2,2,256,256]{3,2,1,0:T(8,128)}, f32[2,2,256,256]{3,2,1,0:T(8,128)S(1)}, f32[2,2,256,256]{3,2,1,0:T(8,128)}, bf16[2,2,2,256,512]{4,3,2,1,0:T(8,128)(2,1)}, bf16[2,2,2,512,256]{4,3,2,1,0:T(8,128)(2,1)}) custom-call(s32[5]{0:T(128)S(1)} %stack.23.refs_0_.place_ref, f32[46,1,256]{2,1,0:T(1,128)S(1)} %get-tuple-element.256.weight_ref, ...), custom_call_target="tpu_custom_call" | custom-call | flops 1000 | bytes 1000 | tf_op jit(solution)/shard_map/pallas_call | solution.py:331
  50.9 1.9 %collective-permute-done.30 = f32[2,256,256]{2,1,0:T(8,128)} collective-permute-done((f32[2,256,256]{2,1,0:T(8,128)}, f32[2,256,256]{2,1,0:T(8,128)}, u32[]{:S(2)}, u32[]{:S(2)}) %collective-permute-start.30) | collective-permute-done | bytes 524320 | tf_op jit(solution)/shard_map/ppermute | solution.py:345
  52.8 18.2 %conditional.1 = (f32[2,2,256,256]{3,2,1,0:T(8,128)}) conditional(s32[]{:T(128)} %bitcast.12, (f32[2,2,256,256]{3,2,1,0:T(8,128)S(1)}, f32[2,256,256]{2,1,0:T(8,128)}, f32[2,256,256]{2,1,0:T(8,128)}, s32[5]{0:T(128)S(1)}, f32[46,1,256]{2,1,0:T(1,128)S(1)}, /*index=5*/bf16[2,2,2,256,512]{4,3,2,1,0:T(8,128)(2,1)}, ...), branch_computations={%region_0.1_spmd, %region_1.2_spmd, %region_2.8_spmd} | conditional | flops 2099292 | bytes 119019704 | solution.py:532
  53.5 1.6 %branch_0_fun.4 = f32[2,256,256]{2,1,0:T(8,128)S(1)} custom-call(f32[15,1,128]{2,1,0:T(1,128)S(1)} %get-tuple-element.154.slot_ref, f32[2,256,256]{2,1,0:T(8,128)} %get-tuple-element.155.refs_0_, f32[2,256,256]{2,1,0:T(8,128)} %get-tuple-element.156.refs_1_, f32[2,256,256]{2,1,0:T(8,128)} %get-tuple-element.157.refs_2_, ...), custom_call_target="tpu_custom_call" | custom-call | flops 1000 | bytes 1000 | tf_op jit(solution)/shard_map/cond/branch_0_fun/pallas_call | solution.py:387
  55.0 1.6 %collective-permute-start.3 = (f32[2,256,256]{2,1,0:T(8,128)S(1)}, f32[2,256,256]{2,1,0:T(8,128)S(1)}, u32[]{:S(2)}, u32[]{:S(2)}) collective-permute-start(f32[2,256,256]{2,1,0:T(8,128)S(1)} %branch_0_fun.4), channel_id=1, source_target_pairs={{0,2},{2,0},{1,3},{3,1},{4,6},{6,4},{5,7},{7,5},{8,10},{10,8},{9,1... | collective-permute-start | bytes 1572872 | tf_op jit(solution)/shard_map/cond/branch_0_fun/ppermute | solution.py:345
  57.3 7.1 %branch_0_fun.3 = (f32[2,2,256,256]{3,2,1,0:T(8,128)S(1)}, bf16[1,2,2,2,256,256]{5,4,3,2,1,0:T(8,128)(2,1)S(1)}) custom-call(s32[5]{0:T(128)S(1)} %get-tuple-element.143.place_ref, f32[46,1,256]{2,1,0:T(1,128)S(1)} %get-tuple-element.142.weight_ref, bf16[2,2,2,256,512]{4,3,2,1,0:T(8,128)(2,1)S(1)} %copy-done.22, bf16[2,2,2,512,256]{4,3,2,1,0:T(8,128)(2,1)S(1)} %copy-done.14, ...), custom_call_target="tpu_custom_call" | custom-call | flops 1000 | bytes 1000 | tf_op jit(solution)/shard_map/cond/branch_0_fun/pallas_call | solution.py:331
  64.4 4.6 %collective-permute-done.3.refs_0_ = f32[2,256,256]{2,1,0:T(8,128)S(1)} collective-permute-done((f32[2,256,256]{2,1,0:T(8,128)S(1)}, f32[2,256,256]{2,1,0:T(8,128)S(1)}, u32[]{:S(2)}, u32[]{:S(2)}) %collective-permute-start.3) | collective-permute-done | bytes 524320 | tf_op jit(solution)/shard_map/cond/branch_0_fun/ppermute | solution.py:345
  69.0 2.0 %branch_0_fun.5 = f32[2,2,256,256]{3,2,1,0:T(8,128)} custom-call(f32[46,1,256]{2,1,0:T(1,128)S(1)} %get-tuple-element.142.weight_ref, f32[2,2,256,256]{3,2,1,0:T(8,128)S(1)} %get-tuple-element.152.sum_ref, bf16[1,2,2,2,256,256]{5,4,3,2,1,0:T(8,128)(2,1)S(1)} %get-tuple-element.153.left_ref, f32[2,256,256]{2,1,0:T(8,128)S(1)} %collective-permute-done.3.refs_0_), custom_call_target="tpu_custom_call" | custom-call | flops 1000 | bytes 1000 | tf_op jit(solution)/shard_map/cond/branch_0_fun/pallas_call | solution.py:331
  71.0 3.0 %shard_map.52.half_ref = f32[2,2,256,256]{3,2,1,0:T(8,128)S(1)} custom-call(s32[5]{0:T(128)S(1)} %stack.23.refs_0_.place_ref, s32[8]{0:T(128)S(1)} %copy-done.8, bf16[2,2,2,512,256]{4,3,2,1,0:T(8,128)(2,1)} %get-tuple-element.276.col_ref, f32[2,2,256,256]{3,2,1,0:T(8,128)} %get-tuple-element.628.s_ref), custom_call_target="tpu_custom_call" | custom-call | flops 1000 | bytes 1000 | tf_op jit(solution)/shard_map/pallas_call | solution.py:331
  74.0 2.5 %shard_map.53 = f32[2,2,256,256]{3,2,1,0:T(8,128)} custom-call(s32[5]{0:T(128)S(1)} %stack.23.refs_0_.place_ref, s32[8]{0:T(128)S(1)} %copy-done.8, bf16[2,2,2,512,256]{4,3,2,1,0:T(8,128)(2,1)S(1)} %copy-done.13, f32[2,2,256,256]{3,2,1,0:T(8,128)S(1)} %shard_map.52.half_ref, f32[2,2,256,256]{3,2,1,0:T(8,128)S(1)} %collective-permute-done.31.refs_0_), custom_call_target="tpu_custom_call" | custom-call | flops 1000 | bytes 1000 | tf_op jit(solution)/shard_map/pallas_call | solution.py:331
  (39 shorter events, 6.5 us)
Async XLA Ops:
  2.9 15.1 %collective-permute-start.20 = (f32[2,256,256]{2,1,0:T(8,128)S(1)}, f32[2,256,256]{2,1,0:T(8,128)}, u32[]{:S(2)}, u32[]{:S(2)}) collective-permute-start(f32[2,256,256]{2,1,0:T(8,128)S(1)} %get-tuple-element.257), channel_id=1, source_target_pairs={{0,4},{8,12},{4,0},{12,8},{1,5},{9,13},{5,1},{13,9},{2,6},{10,14},... | collective-permute-start | bytes 1572872 | tf_op jit(solution)/shard_map/ppermute | solution.py:398
  6.0 12.0 %collective-permute-start.21 = (f32[2,256,256]{2,1,0:T(8,128)S(1)}, f32[2,256,256]{2,1,0:T(8,128)}, u32[]{:S(2)}, u32[]{:S(2)}) collective-permute-start(f32[2,256,256]{2,1,0:T(8,128)S(1)} %get-tuple-element.258), channel_id=1, source_target_pairs={{4,8},{8,4},{5,9},{9,5},{6,10},{10,6},{7,11},{11,7},{20,24},{24,20... | collective-permute-start | bytes 1572872 | tf_op jit(solution)/shard_map/ppermute | solution.py:398
  7.5 15.1 %collective-permute-start.22 = (f32[2,256,256]{2,1,0:T(8,128)}, f32[2,256,256]{2,1,0:T(8,128)S(1)}, u32[]{:S(2)}, u32[]{:S(2)}) collective-permute-start(f32[2,256,256]{2,1,0:T(8,128)} %get-tuple-element.259.refs_0_), channel_id=1, source_target_pairs={{0,2},{2,0},{1,3},{3,1},{4,6},{6,4},{5,7},{7,5},{8,10},{10,8},{9,1... | collective-permute-start | bytes 1572872 | tf_op jit(solution)/shard_map/ppermute | solution.py:345
  9.0 27.6 %collective-permute-start.26 = (f32[2,2,256,256]{3,2,1,0:T(8,128)}, f32[2,2,256,256]{3,2,1,0:T(8,128)S(1)}, u32[]{:S(2)}, u32[]{:S(2)}) collective-permute-start(f32[2,2,256,256]{3,2,1,0:T(8,128)} %refs_0_.1), channel_id=1, source_target_pairs={{0,1},{1,0},{2,3},{3,2},{4,5},{5,4},{6,7},{7,6},{8,9},{9,8},{10,11... | collective-permute-start | bytes 3145736 | tf_op jit(solution)/shard_map/ppermute | solution.py:345
  9.0 23.3 %collective-permute-start.25 = (f32[2,256,256]{2,1,0:T(8,128)}, f32[2,256,256]{2,1,0:T(8,128)S(1)}, u32[]{:S(2)}, u32[]{:S(2)}) collective-permute-start(f32[2,256,256]{2,1,0:T(8,128)} %get-tuple-element.263.refs_1_), channel_id=1, source_target_pairs={{0,2},{2,0},{1,3},{3,1},{4,6},{6,4},{5,7},{7,5},{8,10},{10,8},{9,1... | collective-permute-start | bytes 1572872 | tf_op jit(solution)/shard_map/ppermute | solution.py:345
  12.5 32.2 %copy-start.17 = (f32[2,2,256,256]{3,2,1,0:T(8,128)S(1)}, f32[2,2,256,256]{3,2,1,0:T(8,128)}, u32[]{:S(2)}) copy-start(f32[2,2,256,256]{3,2,1,0:T(8,128)} %refs_0_.1) | copy-start | bytes 3145732
  23.9 28.9 %copy-start.26 = (s32[4,2]{0,1:T(2,128)S(1)}, s32[4,2]{0,1:T(2,128)}, u32[]{:S(2)}) copy-start(s32[4,2]{0,1:T(2,128)} %param.10) | copy-start | bytes 100
  23.9 28.9 %copy-start.27 = (s32[4]{0:T(128)S(1)}, s32[4]{0:T(128)}, u32[]{:S(2)}) copy-start(s32[4]{0:T(128)} %refs_2_.1) | copy-start | bytes 52
  23.9 12.6 %collective-permute-start.23 = (f32[2,256,256]{2,1,0:T(8,128)S(1)}, f32[2,256,256]{2,1,0:T(8,128)S(1)}, u32[]{:S(2)}, u32[]{:S(2)}) collective-permute-start(f32[2,256,256]{2,1,0:T(8,128)S(1)} %get-tuple-element.264), channel_id=1, source_target_pairs={{0,4},{8,12},{4,0},{12,8},{1,5},{9,13},{5,1},{13,9},{2,6},{10,14},... | collective-permute-start | bytes 1572872 | tf_op jit(solution)/shard_map/ppermute | solution.py:398
  27.7 8.8 %collective-permute-start.24 = (f32[2,256,256]{2,1,0:T(8,128)S(1)}, f32[2,256,256]{2,1,0:T(8,128)S(1)}, u32[]{:S(2)}, u32[]{:S(2)}) collective-permute-start(f32[2,256,256]{2,1,0:T(8,128)S(1)} %get-tuple-element.265), channel_id=1, source_target_pairs={{4,8},{8,4},{5,9},{9,5},{6,10},{10,6},{7,11},{11,7},{20,24},{24,20... | collective-permute-start | bytes 1572872 | tf_op jit(solution)/shard_map/ppermute | solution.py:398
  28.4 8.1 %collective-permute-start.27 = (s32[2]{0:T(128)S(1)}, s32[2]{0:T(128)S(1)}, u32[]{:S(2)}, u32[]{:S(2)}) collective-permute-start(s32[2]{0:T(128)S(1)} %get-tuple-element.277.refs_0_), channel_id=1, source_target_pairs={{0,16},{16,0},{1,17},{17,1},{2,18},{18,2},{3,19},{19,3},{4,20},{20... | collective-permute-start | bytes 32 | tf_op jit(solution)/shard_map/ppermute | solution.py:345
  36.5 8.1 %copy-start.20 = (f32[2,256,256]{2,1,0:T(8,128)}, f32[2,256,256]{2,1,0:T(8,128)S(1)}, u32[]{:S(2)}) copy-start(f32[2,256,256]{2,1,0:T(8,128)S(1)} %collective-permute-done.23.refs_6_.refs_4_) | copy-start | bytes 1572868
  36.5 8.1 %copy-start.21 = (f32[2,256,256]{2,1,0:T(8,128)}, f32[2,256,256]{2,1,0:T(8,128)S(1)}, u32[]{:S(2)}) copy-start(f32[2,256,256]{2,1,0:T(8,128)S(1)} %collective-permute-done.24.refs_7_.refs_5_) | copy-start | bytes 1572868
  39.1 11.8 %collective-permute-start.28 = (f32[2,256,256]{2,1,0:T(8,128)}, f32[2,256,256]{2,1,0:T(8,128)}, u32[]{:S(2)}, u32[]{:S(2)}) collective-permute-start(f32[2,256,256]{2,1,0:T(8,128)} %get-tuple-element.280), channel_id=1, source_target_pairs={{0,4},{8,12},{4,0},{12,8},{1,5},{9,13},{5,1},{13,9},{2,6},{10,14},... | collective-permute-start | bytes 1572872 | tf_op jit(solution)/shard_map/ppermute | solution.py:398
  41.7 9.2 %collective-permute-start.29 = (f32[2,256,256]{2,1,0:T(8,128)}, f32[2,256,256]{2,1,0:T(8,128)}, u32[]{:S(2)}, u32[]{:S(2)}) collective-permute-start(f32[2,256,256]{2,1,0:T(8,128)} %get-tuple-element.281), channel_id=1, source_target_pairs={{4,8},{8,4},{5,9},{9,5},{6,10},{10,6},{7,11},{11,7},{20,24},{24,20... | collective-permute-start | bytes 1572872 | tf_op jit(solution)/shard_map/ppermute | solution.py:398
  43.1 9.6 %collective-permute-start.30 = (f32[2,256,256]{2,1,0:T(8,128)}, f32[2,256,256]{2,1,0:T(8,128)}, u32[]{:S(2)}, u32[]{:S(2)}) collective-permute-start(f32[2,256,256]{2,1,0:T(8,128)} %get-tuple-element.282), channel_id=1, source_target_pairs={{0,2},{2,0},{1,3},{3,1},{4,6},{6,4},{5,7},{7,5},{8,10},{10,8},{9,1... | collective-permute-start | bytes 1572872 | tf_op jit(solution)/shard_map/ppermute | solution.py:345
  52.8 18.2 %copy-start.8 = (s32[8]{0:T(128)S(1)}, s32[8]{0:T(128)}, u32[]{:S(2)}) copy-start(s32[8]{0:T(128)} %pick_ref.3) | copy-start | bytes 100
  52.8 4.5 %copy-start.14 = (bf16[2,2,2,512,256]{4,3,2,1,0:T(8,128)(2,1)S(1)}, bf16[2,2,2,512,256]{4,3,2,1,0:T(8,128)(2,1)}, u32[]{:S(2)}) copy-start(bf16[2,2,2,512,256]{4,3,2,1,0:T(8,128)(2,1)} %get-tuple-element.145.col_ref) | copy-start | bytes 6291460 | tf_op jit(solution)/shard_map/cond
  52.8 4.5 %copy-start.22 = (bf16[2,2,2,256,512]{4,3,2,1,0:T(8,128)(2,1)S(1)}, bf16[2,2,2,256,512]{4,3,2,1,0:T(8,128)(2,1)}, u32[]{:S(2)}) copy-start(bf16[2,2,2,256,512]{4,3,2,1,0:T(8,128)(2,1)} %get-tuple-element.144.row_ref) | copy-start | bytes 6291460 | tf_op jit(solution)/shard_map/cond
  52.8 4.4 %collective-permute-start = (f32[2,2,256,256]{3,2,1,0:T(8,128)S(1)}, f32[2,2,256,256]{3,2,1,0:T(8,128)S(1)}, u32[]{:S(2)}, u32[]{:S(2)}) collective-permute-start(f32[2,2,256,256]{3,2,1,0:T(8,128)S(1)} %get-tuple-element.148.refs_2_), channel_id=1, source_target_pairs={{0,1},{1,0},{2,3},{3,2},{4,5},{5,4},{6,7},{7,6},{8,9},{9,8},{10,11... | collective-permute-start | bytes 3145736 | tf_op jit(solution)/shard_map/cond/branch_0_fun/ppermute | solution.py:345
  52.9 3.7 %collective-permute-start.1 = (f32[2,256,256]{2,1,0:T(8,128)}, f32[2,256,256]{2,1,0:T(8,128)S(1)}, u32[]{:S(2)}, u32[]{:S(2)}) collective-permute-start(f32[2,256,256]{2,1,0:T(8,128)} %get-tuple-element.149.refs_4_.refs_6_), channel_id=1, source_target_pairs={{0,1},{1,0},{2,3},{3,2},{4,5},{5,4},{6,7},{7,6},{8,9},{9,8},{10,11... | collective-permute-start | bytes 1572872 | tf_op jit(solution)/shard_map/cond/branch_0_fun/ppermute | solution.py:345
  53.4 3.9 %collective-permute-start.2 = (f32[2,256,256]{2,1,0:T(8,128)}, f32[2,256,256]{2,1,0:T(8,128)S(1)}, u32[]{:S(2)}, u32[]{:S(2)}) collective-permute-start(f32[2,256,256]{2,1,0:T(8,128)} %get-tuple-element.150.refs_5_.refs_7_), channel_id=1, source_target_pairs={{0,1},{1,0},{2,3},{3,2},{4,5},{5,4},{6,7},{7,6},{8,9},{9,8},{10,11... | collective-permute-start | bytes 1572872 | tf_op jit(solution)/shard_map/cond/branch_0_fun/ppermute | solution.py:345
  55.0 13.9 %collective-permute-start.3 = (f32[2,256,256]{2,1,0:T(8,128)S(1)}, f32[2,256,256]{2,1,0:T(8,128)S(1)}, u32[]{:S(2)}, u32[]{:S(2)}) collective-permute-start(f32[2,256,256]{2,1,0:T(8,128)S(1)} %branch_0_fun.4), channel_id=1, source_target_pairs={{0,2},{2,0},{1,3},{3,1},{4,6},{6,4},{5,7},{7,5},{8,10},{10,8},{9,1... | collective-permute-start | bytes 1572872 | tf_op jit(solution)/shard_map/cond/branch_0_fun/ppermute | solution.py:345
  70.9 3.0 %collective-permute-start.31 = (f32[2,2,256,256]{3,2,1,0:T(8,128)}, f32[2,2,256,256]{3,2,1,0:T(8,128)S(1)}, u32[]{:S(2)}, u32[]{:S(2)}) collective-permute-start(f32[2,2,256,256]{3,2,1,0:T(8,128)} %get-tuple-element.628.s_ref), channel_id=1, source_target_pairs={{0,1},{1,0},{2,3},{3,2},{4,5},{5,4},{6,7},{7,6},{8,9},{9,8},{10,11... | collective-permute-start | bytes 3145736 | tf_op jit(solution)/shard_map/ppermute | solution.py:345
  (1 other events, 3.0 us)
where the time goes:
time: 77.3 us; the launch traced here: 76.5 us
  Pallas kernels  31.5 us (41%)
  waiting for transfers between devices  23.8 us (31%)
  starting transfers between devices  20.3 us (26%)
    pallas_call x5, Pallas kernels, call(): pl.pallas_call(kernel, out_shape=outs, in_specs=[pl.BlockSpec(memory_spac...  19.2 us
    ppermute x10, waiting for transfers between devices, shifts(): lax.ppermute(array, axis, [(i, (i + j) % size) for i in range(size)])  14 us
    ppermute x6, starting transfers between devices, meet(): lax.ppermute(item, 'node', swap)  13.1 us
    ppermute x6, waiting for transfers between devices, meet(): lax.ppermute(item, 'node', swap)  9.77 us
    ppermute x10, starting transfers between devices, shifts(): lax.ppermute(array, axis, [(i, (i + j) % size) for i in range(size)])  7.22 us
    pallas_call x3, Pallas kernels, choose(): pl.pallas_call(functools.partial(choose_kernel, [3 * step + kind for kind...  5.47 us
    pallas_call x1, Pallas kernels, plan_rounds(): pl.pallas_call(functools.partial(plan_kernel, line, owned, term_nodes.sha...  2.97 us
    pallas_call x1, Pallas kernels, body(): pl.pallas_call(functools.partial(first_kernel, line, owned, terms), out_s...  2.83 us
  transfers between devices with their start and end apart: 16, of which 7 were waited for; matrix products, arithmetic and copies ran while one was open for 0% of the time, Pallas kernels for 28%

commit v1 on v0

--- a/solution.py
+++ b/solution.py
@@ -62,15 +62,21 @@
         slot_ref[row] = jnp.broadcast_to(slot, slot_ref.shape[1:])
         return wanted_name
 
+    def second_for(side):
+        return jnp.max(jnp.where(side, wanted, 0.0), axis=0, keepdims=True).astype(jnp.int32)
+
+    left_second, right_second = second_for(place < home), second_for(place > home)
     left, right = home, home
     lane = lax.broadcasted_iota(jnp.int32, (line, 2), 1)
     length = jnp.zeros((line, 2), jnp.int32)
     gone = []
     for step in range(rounds):
         to_go = jnp.where((left == place) & (lowest < place), place - lowest, 0)
-        best_left, moved_left, send_left = pick(jnp.where(to_go > 0, (to_go + 1) * count - ids, 0).astype(jnp.float32))
+        score = jnp.where(to_go > 0, (2 * to_go + left_second + 1) * count - ids, 0)
+        best_left, moved_left, send_left = pick(score.astype(jnp.float32))
         to_go = jnp.where((right == place) & (highest > place), highest - place, 0)
-        best_right, moved_right, send_right = pick(jnp.where(to_go > 0, (to_go + 1) * count - ids, 0).astype(jnp.float32))
+        score = jnp.where(to_go > 0, (2 * to_go + right_second + 1) * count - ids, 0)
+        best_right, moved_right, send_right = pick(score.astype(jnp.float32))
         busy_line = jnp.max(jnp.maximum(best_left, best_right), axis=0, keepdims=True)
         if step >= FIRST_OVER:
             here = ((left <= place) & (place < home)) | ((right >= place) & (place > home))
@@ -197,7 +203,8 @@
     fetch.wait()
     me = place_ref[0]
     choice = []
-    lows, highs = [jnp.int32(0)] * owned, [jnp.int32(0)] * owned
+    zero = jnp.int32(0)
+    lows, highs, low_seconds, high_seconds = [[zero] * owned for _ in range(4)]
     for t in range(terms):
         a, b = terms_here[0, t], terms_here[1, t]
         to_second, to_first = b // owned - me, a // owned - me
@@ -206,11 +213,14 @@
             away = jnp.where(a == name, to_second, jnp.where(b == name, to_first, 0))
             lows[m] = jnp.maximum(lows[m], -away)
             highs[m] = jnp.maximum(highs[m], away)
-    for far in (lows, highs):
-        best, slot = far[0], jnp.int32(0)
-        for m in range(1, owned):
-            slot = jnp.where(far[m] > best, m, slot)
-            best = jnp.maximum(far[m], best)
+            low_seconds[m] = jnp.where((b == name) & (to_first < 0), 1, low_seconds[m])
+            high_seconds[m] = jnp.where((b == name) & (to_first > 0), 1, high_seconds[m])
+    for far, seconds in ((lows, low_seconds), (highs, high_seconds)):
+        best, slot = jnp.int32(-1), zero
+        for m in range(owned):
+            score = jnp.where(far[m] > 0, 2 * far[m] + seconds[m], 0)
+            slot = jnp.where(score > best, m, slot)
+            best = jnp.maximum(score, best)
         choice.append(slot)
     even = lax.rem(me, 2) == 0
     slots = (jnp.where(even, choice[1], choice[0]), jnp.where(even, choice[0], choice[1]))
@@ -321,10 +331,13 @@
 
 def way_kernel(groups, fixed, *refs):
     lengths, out_ref = refs[:groups], refs[groups]
-    way = jnp.int32(0)
+    along, over = jnp.int32(0), jnp.int32(0)
     for length in lengths:
-        way = jnp.maximum(way, jnp.maximum(length[0] - fixed, length[1] - fixed - 1))
-    out_ref[0] = jnp.minimum(way, 2)
+        along = jnp.maximum(along, length[0] - fixed)
+        over = jnp.maximum(over, length[1] - fixed - 1)
+    way = jnp.where(along > 0, 1, 0)
+    way = jnp.where(over > 0, 2, way)
+    out_ref[0] = jnp.where((along > 1) | (over > 1), 3, way)
 
 
 def call(kernel, scalars, arrays, outs, scratch=()):
@@ -467,26 +480,34 @@
 
     u, *ux = early[:1] + early[2:]
 
+    def level(came, over):
+        v = [early[1], *shifts(early[1], "rep")]
+        return sums(row, col, [u, *ux], v, beyond_rep(came[before:]), over)
+
     def end(step, came, over):
         [item] = choose(step, (2,), came)
         late = shifts(item, "sub")
-        fresh = beyond_rep(came[before:])
-        v = [early[1], *shifts(early[1], "rep")]
         first = 2 * owned * names + step - FIRST_OVER
         return call(
             functools.partial(late_kernel, subs, first, gone),
             [],
-            [weights, *sums(row, col, [u, *ux], v, fresh, over), *late],
+            [weights, *level(came, over), *late],
             out(nodes_shape),
         )
 
     def short(_):
         return end(fixed, came, over)
 
-    def middle(_):
+    def one_more():
         first, second, item = choose(fixed, (0, 1, 2), came)
         new, beyond = lax.optimization_barrier((meet(first, second), shifts(item, "sub")))
-        return end(fixed + 1, came + new, over + beyond)
+        return came + new, over + beyond
+
+    def middle(_):
+        return level(*one_more())[0]
+
+    def middle_end(_):
+        return end(fixed + 1, *one_more())
 
     def long(_):
         edges = jnp.pad(tables.reshape(-1, 3, line), ((0, 0), (0, 0), (1, 1)), constant_values=count)
@@ -529,7 +550,7 @@
         _, _, u, v = lax.while_loop(more, again, (jnp.int32(0), held, [u, *ux], v))
         return sums(row, col, u, [v, *shifts(v, "rep")])[0]
 
-    summed = lax.switch(way[0], [short, middle, long], None)
+    summed = lax.switch(way[0], [short, middle, middle_end, long], None)
     half = call(functools.partial(half_kernel, subs), [place, resident_pick], [col, summed], out(meson_nodes.shape))
     return call(
         functools.partial(last_kernel, subs),

time: 77.3 us -> 85.6 us (1.11)
  starting transfers between devices: 20.3 us -> 25.6 us
  waiting for transfers between devices: 23.8 us -> 27.8 us
  Pallas kernels: 31.5 us -> 30.6 us
    ppermute x6 -> x8, starting transfers between devices: 13.1 us -> 17.8 us  [meet(): lax.ppermute(item, 'node', swap)]
    ppermute x6 -> x8, waiting for transfers between devices: 9.77 us -> 13.9 us  [meet(): lax.ppermute(item, 'node', swap)]
    pallas_call x3, Pallas kernels: 5.47 us -> 4.54 us  [choose(): pl.pallas_call(functools.partial(choose_kernel, [3 * step + kind for kind...]
    ppermute x10 -> x12, starting transfers between devices: 7.22 us -> 7.82 us  [shifts(): lax.ppermute(array, axis, [(i, (i + j) % size) for i in range(size)])]
    ppermute x10 -> x12, waiting for transfers between devices: 14 us -> 13.9 us  [shifts(): lax.ppermute(array, axis, [(i, (i + j) % size) for i in range(size)])]
    pallas_call x5 -> x4, Pallas kernels: 19.2 us -> 19.2 us  [call(): pl.pallas_call(kernel, out_shape=outs, in_specs=[pl.BlockSpec(memory_spac...]
  transfers between devices with their start and end apart: 16 -> 20, of which waited for: 7 -> 9; matrix products, arithmetic and copies ran while one was open for 0% -> 0% of each run, Pallas kernels for 28% -> 15%
where the time goes in v1:
time: 85.6 us; the launch traced here: 85 us
  Pallas kernels  30.6 us (36%)
  waiting for transfers between devices  27.8 us (32%)
  starting transfers between devices  25.6 us (30%)
    pallas_call x4, Pallas kernels, call(): pl.pallas_call(kernel, out_shape=outs, in_specs=[pl.BlockSpec(memory_spac...  19.2 us
    ppermute x8, starting transfers between devices, meet(): lax.ppermute(item, 'node', swap)  17.8 us
    ppermute x8, waiting for transfers between devices, meet(): lax.ppermute(item, 'node', swap)  13.9 us
    ppermute x12, waiting for transfers between devices, shifts(): lax.ppermute(array, axis, [(i, (i + j) % size) for i in range(size)])  13.9 us
    ppermute x12, starting transfers between devices, shifts(): lax.ppermute(array, axis, [(i, (i + j) % size) for i in range(size)])  7.82 us
    pallas_call x3, Pallas kernels, choose(): pl.pallas_call(functools.partial(choose_kernel, [3 * step + kind for kind...  4.54 us
    pallas_call x1, Pallas kernels, plan_rounds(): pl.pallas_call(functools.partial(plan_kernel, line, owned, term_nodes.sha...  3 us
    pallas_call x1, Pallas kernels, body(): pl.pallas_call(functools.partial(first_kernel, line, owned, terms), out_s...  2.84 us
  transfers between devices with their start and end apart: 20, of which 9 were waited for; matrix products, arithmetic and copies ran while one was open for 0% of the time, Pallas kernels for 15%

profile of v1, /device:TPU:0, one launch (start us, length us, event | category | flops | bytes accessed | tf_op | source)
XLA Modules:
  0.0 85.0 jit_solution(6290399021306806291)
XLA Ops:
  0.1 2.8 %shard_map.47 = (f32[2,256,256]{2,1,0:T(8,128)S(1)}, f32[2,256,256]{2,1,0:T(8,128)S(1)}, f32[2,256,256]{2,1,0:T(8,128)}, f32[2,256,256]{2,1,0:T(8,128)}) custom-call(s32[5]{0:T(128)S(1)} %stack.23.refs_0_.place_ref, s32[2,4]{1,0:T(2,128)} %bitcast.55, f32[2,2,256,256]{3,2,1,0:T(8,128)} %refs_0_.1), custom_call_target="tpu_custom_call" | custom-call | flops 1000 | bytes 1000 | tf_op jit(solution)/shard_map/pallas_call | solution.py:413
  2.9 3.1 %collective-permute-start.28 = (f32[2,256,256]{2,1,0:T(8,128)S(1)}, f32[2,256,256]{2,1,0:T(8,128)}, u32[]{:S(2)}, u32[]{:S(2)}) collective-permute-start(f32[2,256,256]{2,1,0:T(8,128)S(1)} %get-tuple-element.316), channel_id=1, source_target_pairs={{0,4},{8,12},{4,0},{12,8},{1,5},{9,13},{5,1},{13,9},{2,6},{10,14},... | collective-permute-start | bytes 1572872 | tf_op jit(solution)/shard_map/ppermute | solution.py:411
  7.5 1.5 %collective-permute-start.30 = (f32[2,256,256]{2,1,0:T(8,128)}, f32[2,256,256]{2,1,0:T(8,128)S(1)}, u32[]{:S(2)}, u32[]{:S(2)}) collective-permute-start(f32[2,256,256]{2,1,0:T(8,128)} %get-tuple-element.318.refs_0_), channel_id=1, source_target_pairs={{0,2},{2,0},{1,3},{3,1},{4,6},{6,4},{5,7},{7,5},{8,10},{10,8},{9,1... | collective-permute-start | bytes 1572872 | tf_op jit(solution)/shard_map/ppermute | solution.py:358
  9.5 3.0 %shard_map.46 = (f32[15,1,128]{2,1,0:T(1,128)S(1)}, f32[46,1,256]{2,1,0:T(1,128)S(1)}, s32[27,4,1]{2,1,0:T(4,128)S(1)}, s32[2]{0:T(128)S(1)}) custom-call(s32[5]{0:T(128)S(1)} %stack.23.refs_0_.place_ref, s32[2,4]{1,0:T(2,128)} %bitcast.56, s32[4]{0:T(128)} %refs_2_.1), custom_call_target="tpu_custom_call" | custom-call | flops 1000 | bytes 1000 | tf_op jit(solution)/shard_map/pallas_call | solution.py:124
  12.5 5.5 %collective-permute-done.28.refs_2_.refs_4_ = f32[2,256,256]{2,1,0:T(8,128)} collective-permute-done((f32[2,256,256]{2,1,0:T(8,128)S(1)}, f32[2,256,256]{2,1,0:T(8,128)}, u32[]{:S(2)}, u32[]{:S(2)}) %collective-permute-start.28) | collective-permute-done | bytes 524320 | tf_op jit(solution)/shard_map/ppermute | solution.py:411
  18.1 4.5 %collective-permute-done.30.refs_2_ = f32[2,256,256]{2,1,0:T(8,128)S(1)} collective-permute-done((f32[2,256,256]{2,1,0:T(8,128)}, f32[2,256,256]{2,1,0:T(8,128)S(1)}, u32[]{:S(2)}, u32[]{:S(2)}) %collective-permute-start.30) | collective-permute-done | bytes 524320 | tf_op jit(solution)/shard_map/ppermute | solution.py:358
  23.9 3.7 %collective-permute-start.31 = (f32[2,256,256]{2,1,0:T(8,128)S(1)}, f32[2,256,256]{2,1,0:T(8,128)S(1)}, u32[]{:S(2)}, u32[]{:S(2)}) collective-permute-start(f32[2,256,256]{2,1,0:T(8,128)S(1)} %get-tuple-element.323), channel_id=1, source_target_pairs={{0,4},{8,12},{4,0},{12,8},{1,5},{9,13},{5,1},{13,9},{2,6},{10,14},... | collective-permute-start | bytes 1572872 | tf_op jit(solution)/shard_map/ppermute | solution.py:411
  28.3 1.6 %collective-permute-start.35 = (s32[2]{0:T(128)S(1)}, s32[2]{0:T(128)S(1)}, u32[]{:S(2)}, u32[]{:S(2)}) collective-permute-start(s32[2]{0:T(128)S(1)} %get-tuple-element.336.refs_0_), channel_id=1, source_target_pairs={{0,16},{16,0},{1,17},{17,1},{2,18},{18,2},{3,19},{19,3},{4,20},{20... | collective-permute-start | bytes 32 | tf_op jit(solution)/shard_map/ppermute | solution.py:358
  29.9 2.4 %collective-permute-done.33.refs_3_ = f32[2,256,256]{2,1,0:T(8,128)S(1)} collective-permute-done((f32[2,256,256]{2,1,0:T(8,128)}, f32[2,256,256]{2,1,0:T(8,128)S(1)}, u32[]{:S(2)}, u32[]{:S(2)}) %collective-permute-start.33) | collective-permute-done | bytes 524320 | tf_op jit(solution)/shard_map/ppermute | solution.py:358
  32.3 4.1 %collective-permute-done.31.refs_6_.refs_4_ = f32[2,256,256]{2,1,0:T(8,128)S(1)} collective-permute-done((f32[2,256,256]{2,1,0:T(8,128)S(1)}, f32[2,256,256]{2,1,0:T(8,128)S(1)}, u32[]{:S(2)}, u32[]{:S(2)}) %collective-permute-start.31) | collective-permute-done | bytes 524320 | tf_op jit(solution)/shard_map/ppermute | solution.py:411
  36.5 1.5 %shard_map.51 = (f32[2,256,256]{2,1,0:T(8,128)}, f32[2,256,256]{2,1,0:T(8,128)}, f32[2,256,256]{2,1,0:T(8,128)}) custom-call(f32[15,1,128]{2,1,0:T(1,128)S(1)} %get-tuple-element.321.slot_ref, f32[2,256,256]{2,1,0:T(8,128)} %get-tuple-element.318.refs_0_, f32[2,256,256]{2,1,0:T(8,128)} %get-tuple-element.322.refs_1_, ...), custom_call_target="tpu_custom_call" | custom-call | flops 1000 | bytes 1000 | tf_op jit(solution)/shard_map/pallas_call | solution.py:400
  37.9 3.7 %collective-permute-start.36 = (f32[2,256,256]{2,1,0:T(8,128)}, f32[2,256,256]{2,1,0:T(8,128)}, u32[]{:S(2)}, u32[]{:S(2)}) collective-permute-start(f32[2,256,256]{2,1,0:T(8,128)} %get-tuple-element.339), channel_id=1, source_target_pairs={{0,4},{8,12},{4,0},{12,8},{1,5},{9,13},{5,1},{13,9},{2,6},{10,14},... | collective-permute-start | bytes 1572872 | tf_op jit(solution)/shard_map/ppermute | solution.py:411
  43.1 1.5 %collective-permute-start.38 = (f32[2,256,256]{2,1,0:T(8,128)}, f32[2,256,256]{2,1,0:T(8,128)}, u32[]{:S(2)}, u32[]{:S(2)}) collective-permute-start(f32[2,256,256]{2,1,0:T(8,128)} %get-tuple-element.341), channel_id=1, source_target_pairs={{0,2},{2,0},{1,3},{3,1},{4,6},{6,4},{5,7},{7,5},{8,10},{10,8},{9,1... | collective-permute-start | bytes 1572872 | tf_op jit(solution)/shard_map/ppermute | solution.py:358
  44.6 4.5 %shard_map.49 = (f32[2,2,256,256]{3,2,1,0:T(8,128)}, f32[2,2,256,256]{3,2,1,0:T(8,128)S(1)}, f32[2,2,256,256]{3,2,1,0:T(8,128)}, bf16[2,2,2,256,512]{4,3,2,1,0:T(8,128)(2,1)}, bf16[2,2,2,512,256]{4,3,2,1,0:T(8,128)(2,1)}) custom-call(s32[5]{0:T(128)S(1)} %stack.23.refs_0_.place_ref, f32[46,1,256]{2,1,0:T(1,128)S(1)} %get-tuple-element.315.weight_ref, ...), custom_call_target="tpu_custom_call" | custom-call | flops 1000 | bytes 1000 | tf_op jit(solution)/shard_map/pallas_call | solution.py:344
  50.7 2.0 %collective-permute-done.38 = f32[2,256,256]{2,1,0:T(8,128)} collective-permute-done((f32[2,256,256]{2,1,0:T(8,128)}, f32[2,256,256]{2,1,0:T(8,128)}, u32[]{:S(2)}, u32[]{:S(2)}) %collective-permute-start.38) | collective-permute-done | bytes 524320 | tf_op jit(solution)/shard_map/ppermute | solution.py:358
  52.7 26.6 %conditional.1 = (f32[2,2,256,256]{3,2,1,0:T(8,128)}) conditional(s32[]{:T(128)} %bitcast.12, (f32[2,2,256,256]{3,2,1,0:T(8,128)S(1)}, f32[2,256,256]{2,1,0:T(8,128)}, f32[2,256,256]{2,1,0:T(8,128)}, s32[5]{0:T(128)S(1)}, f32[46,1,256]{2,1,0:T(1,128)S(1)}, /*index=5*/bf16[2,2,2,256,512]{4,3,2,1,0:T(8,128)(2,1)}, ...), branch_computations={%region_0.1_spmd, %region_1.2_spmd, %region_2.3_spmd, %region_3.9_... | conditional | flops 2099292 | bytes 119019704 | solution.py:553
  52.7 1.7 %branch_1_fun.2 = (f32[2,256,256]{2,1,0:T(8,128)S(1)}, f32[2,256,256]{2,1,0:T(8,128)S(1)}, f32[2,256,256]{2,1,0:T(8,128)S(1)}) custom-call(f32[15,1,128]{2,1,0:T(1,128)S(1)} %get-tuple-element.205.slot_ref, f32[2,256,256]{2,1,0:T(8,128)} %get-tuple-element.206.refs_0_, f32[2,256,256]{2,1,0:T(8,128)} %get-tuple-element.207.refs_1_, ...), custom_call_target="tpu_custom_call" | custom-call | flops 1000 | bytes 1000 | tf_op jit(solution)/shard_map/cond/branch_1_fun/pallas_call | solution.py:400
  54.5 2.9 %collective-permute-start.5 = (f32[2,256,256]{2,1,0:T(8,128)S(1)}, f32[2,256,256]{2,1,0:T(8,128)S(1)}, u32[]{:S(2)}, u32[]{:S(2)}) collective-permute-start(f32[2,256,256]{2,1,0:T(8,128)S(1)} %get-tuple-element.212), channel_id=1, source_target_pairs={{0,4},{8,12},{4,0},{12,8},{1,5},{9,13},{5,1},{13,9},{2,6},{10,14},... | collective-permute-start | bytes 1572872 | tf_op jit(solution)/shard_map/cond/branch_1_fun/ppermute | solution.py:411
  58.2 1.6 %collective-permute-start.7 = (f32[2,256,256]{2,1,0:T(8,128)S(1)}, f32[2,256,256]{2,1,0:T(8,128)S(1)}, u32[]{:S(2)}, u32[]{:S(2)}) collective-permute-start(f32[2,256,256]{2,1,0:T(8,128)S(1)} %get-tuple-element.214), channel_id=1, source_target_pairs={{0,2},{2,0},{1,3},{3,1},{4,6},{6,4},{5,7},{7,5},{8,10},{10,8},{9,1... | collective-permute-start | bytes 1572872 | tf_op jit(solution)/shard_map/cond/branch_1_fun/ppermute | solution.py:358
  60.3 4.3 %collective-permute-done.5.refs_6_ = f32[2,256,256]{2,1,0:T(8,128)S(1)} collective-permute-done((f32[2,256,256]{2,1,0:T(8,128)S(1)}, f32[2,256,256]{2,1,0:T(8,128)S(1)}, u32[]{:S(2)}, u32[]{:S(2)}) %collective-permute-start.5) | collective-permute-done | bytes 524320 | tf_op jit(solution)/shard_map/cond/branch_1_fun/ppermute | solution.py:411
  64.6 2.9 %collective-permute-done.7.refs_13_ = f32[2,256,256]{2,1,0:T(8,128)S(1)} collective-permute-done((f32[2,256,256]{2,1,0:T(8,128)S(1)}, f32[2,256,256]{2,1,0:T(8,128)S(1)}, u32[]{:S(2)}, u32[]{:S(2)}) %collective-permute-start.7) | collective-permute-done | bytes 524320 | tf_op jit(solution)/shard_map/cond/branch_1_fun/ppermute | solution.py:358
  70.1 9.2 %branch_1_fun.3 = (f32[2,2,256,256]{3,2,1,0:T(8,128)}, bf16[1,2,2,2,256,256]{5,4,3,2,1,0:T(8,128)(2,1)}) custom-call(s32[5]{0:T(128)S(1)} %get-tuple-element.196.place_ref, f32[46,1,256]{2,1,0:T(1,128)S(1)} %get-tuple-element.197.weight_ref, bf16[2,2,2,256,512]{4,3,2,1,0:T(8,128)(2,1)S(1)} %copy-done.22, bf16[2,2,2,512,256]{4,3,2,1,0:T(8,128)(2,1)S(1)} %copy-done.11, ...), custom_call_target="tpu_custom_call" | custom-call | flops 1000 | bytes 1000 | tf_op jit(solution)/shard_map/cond/branch_1_fun/pallas_call | solution.py:344
  79.5 3.0 %shard_map.52.half_ref = f32[2,2,256,256]{3,2,1,0:T(8,128)S(1)} custom-call(s32[5]{0:T(128)S(1)} %stack.23.refs_0_.place_ref, s32[8]{0:T(128)S(1)} %copy-done.8, bf16[2,2,2,512,256]{4,3,2,1,0:T(8,128)(2,1)} %get-tuple-element.335.col_ref, f32[2,2,256,256]{3,2,1,0:T(8,128)} %get-tuple-element.687.s_ref), custom_call_target="tpu_custom_call" | custom-call | flops 1000 | bytes 1000 | tf_op jit(solution)/shard_map/pallas_call | solution.py:344
  82.5 2.5 %shard_map.53 = f32[2,2,256,256]{3,2,1,0:T(8,128)} custom-call(s32[5]{0:T(128)S(1)} %stack.23.refs_0_.place_ref, s32[8]{0:T(128)S(1)} %copy-done.8, bf16[2,2,2,512,256]{4,3,2,1,0:T(8,128)(2,1)S(1)} %copy-done.9, f32[2,2,256,256]{3,2,1,0:T(8,128)S(1)} %shard_map.52.half_ref, f32[2,2,256,256]{3,2,1,0:T(8,128)S(1)} %collective-permute-done.39.refs_0_), custom_call_target="tpu_custom_call" | custom-call | flops 1000 | bytes 1000 | tf_op jit(solution)/shard_map/pallas_call | solution.py:344
  (46 shorter events, 10.9 us)
Async XLA Ops:
  2.9 15.1 %collective-permute-start.28 = (f32[2,256,256]{2,1,0:T(8,128)S(1)}, f32[2,256,256]{2,1,0:T(8,128)}, u32[]{:S(2)}, u32[]{:S(2)}) collective-permute-start(f32[2,256,256]{2,1,0:T(8,128)S(1)} %get-tuple-element.316), channel_id=1, source_target_pairs={{0,4},{8,12},{4,0},{12,8},{1,5},{9,13},{5,1},{13,9},{2,6},{10,14},... | collective-permute-start | bytes 1572872 | tf_op jit(solution)/shard_map/ppermute | solution.py:411
  6.0 12.0 %collective-permute-start.29 = (f32[2,256,256]{2,1,0:T(8,128)S(1)}, f32[2,256,256]{2,1,0:T(8,128)}, u32[]{:S(2)}, u32[]{:S(2)}) collective-permute-start(f32[2,256,256]{2,1,0:T(8,128)S(1)} %get-tuple-element.317), channel_id=1, source_target_pairs={{4,8},{8,4},{5,9},{9,5},{6,10},{10,6},{7,11},{11,7},{20,24},{24,20... | collective-permute-start | bytes 1572872 | tf_op jit(solution)/shard_map/ppermute | solution.py:411
  7.5 15.1 %collective-permute-start.30 = (f32[2,256,256]{2,1,0:T(8,128)}, f32[2,256,256]{2,1,0:T(8,128)S(1)}, u32[]{:S(2)}, u32[]{:S(2)}) collective-permute-start(f32[2,256,256]{2,1,0:T(8,128)} %get-tuple-element.318.refs_0_), channel_id=1, source_target_pairs={{0,2},{2,0},{1,3},{3,1},{4,6},{6,4},{5,7},{7,5},{8,10},{10,8},{9,1... | collective-permute-start | bytes 1572872 | tf_op jit(solution)/shard_map/ppermute | solution.py:358
  9.0 27.5 %collective-permute-start.34 = (f32[2,2,256,256]{3,2,1,0:T(8,128)}, f32[2,2,256,256]{3,2,1,0:T(8,128)S(1)}, u32[]{:S(2)}, u32[]{:S(2)}) collective-permute-start(f32[2,2,256,256]{3,2,1,0:T(8,128)} %refs_0_.1), channel_id=1, source_target_pairs={{0,1},{1,0},{2,3},{3,2},{4,5},{5,4},{6,7},{7,6},{8,9},{9,8},{10,11... | collective-permute-start | bytes 3145736 | tf_op jit(solution)/shard_map/ppermute | solution.py:358
  9.0 23.3 %collective-permute-start.33 = (f32[2,256,256]{2,1,0:T(8,128)}, f32[2,256,256]{2,1,0:T(8,128)S(1)}, u32[]{:S(2)}, u32[]{:S(2)}) collective-permute-start(f32[2,256,256]{2,1,0:T(8,128)} %get-tuple-element.322.refs_1_), channel_id=1, source_target_pairs={{0,2},{2,0},{1,3},{3,1},{4,6},{6,4},{5,7},{7,5},{8,10},{10,8},{9,1... | collective-permute-start | bytes 1572872 | tf_op jit(solution)/shard_map/ppermute | solution.py:358
  12.5 32.0 %copy-start.18 = (f32[2,2,256,256]{3,2,1,0:T(8,128)S(1)}, f32[2,2,256,256]{3,2,1,0:T(8,128)}, u32[]{:S(2)}) copy-start(f32[2,2,256,256]{3,2,1,0:T(8,128)} %refs_0_.1) | copy-start | bytes 3145732
  23.9 28.8 %copy-start.28 = (s32[4,2]{0,1:T(2,128)S(1)}, s32[4,2]{0,1:T(2,128)}, u32[]{:S(2)}) copy-start(s32[4,2]{0,1:T(2,128)} %param.11) | copy-start | bytes 100
  23.9 28.8 %copy-start.29 = (s32[4]{0:T(128)S(1)}, s32[4]{0:T(128)}, u32[]{:S(2)}) copy-start(s32[4]{0:T(128)} %refs_2_.1) | copy-start | bytes 52
  23.9 12.5 %collective-permute-start.31 = (f32[2,256,256]{2,1,0:T(8,128)S(1)}, f32[2,256,256]{2,1,0:T(8,128)S(1)}, u32[]{:S(2)}, u32[]{:S(2)}) collective-permute-start(f32[2,256,256]{2,1,0:T(8,128)S(1)} %get-tuple-element.323), channel_id=1, source_target_pairs={{0,4},{8,12},{4,0},{12,8},{1,5},{9,13},{5,1},{13,9},{2,6},{10,14},... | collective-permute-start | bytes 1572872 | tf_op jit(solution)/shard_map/ppermute | solution.py:411
  27.7 8.8 %collective-permute-start.32 = (f32[2,256,256]{2,1,0:T(8,128)S(1)}, f32[2,256,256]{2,1,0:T(8,128)S(1)}, u32[]{:S(2)}, u32[]{:S(2)}) collective-permute-start(f32[2,256,256]{2,1,0:T(8,128)S(1)} %get-tuple-element.324), channel_id=1, source_target_pairs={{4,8},{8,4},{5,9},{9,5},{6,10},{10,6},{7,11},{11,7},{20,24},{24,20... | collective-permute-start | bytes 1572872 | tf_op jit(solution)/shard_map/ppermute | solution.py:411
  28.3 8.1 %collective-permute-start.35 = (s32[2]{0:T(128)S(1)}, s32[2]{0:T(128)S(1)}, u32[]{:S(2)}, u32[]{:S(2)}) collective-permute-start(s32[2]{0:T(128)S(1)} %get-tuple-element.336.refs_0_), channel_id=1, source_target_pairs={{0,16},{16,0},{1,17},{17,1},{2,18},{18,2},{3,19},{19,3},{4,20},{20... | collective-permute-start | bytes 32 | tf_op jit(solution)/shard_map/ppermute | solution.py:358
  37.9 12.8 %collective-permute-start.36 = (f32[2,256,256]{2,1,0:T(8,128)}, f32[2,256,256]{2,1,0:T(8,128)}, u32[]{:S(2)}, u32[]{:S(2)}) collective-permute-start(f32[2,256,256]{2,1,0:T(8,128)} %get-tuple-element.339), channel_id=1, source_target_pairs={{0,4},{8,12},{4,0},{12,8},{1,5},{9,13},{5,1},{13,9},{2,6},{10,14},... | collective-permute-start | bytes 1572872 | tf_op jit(solution)/shard_map/ppermute | solution.py:411
  41.6 9.1 %collective-permute-start.37 = (f32[2,256,256]{2,1,0:T(8,128)}, f32[2,256,256]{2,1,0:T(8,128)}, u32[]{:S(2)}, u32[]{:S(2)}) collective-permute-start(f32[2,256,256]{2,1,0:T(8,128)} %get-tuple-element.340), channel_id=1, source_target_pairs={{4,8},{8,4},{5,9},{9,5},{6,10},{10,6},{7,11},{11,7},{20,24},{24,20... | collective-permute-start | bytes 1572872 | tf_op jit(solution)/shard_map/ppermute | solution.py:411
  43.1 9.6 %collective-permute-start.38 = (f32[2,256,256]{2,1,0:T(8,128)}, f32[2,256,256]{2,1,0:T(8,128)}, u32[]{:S(2)}, u32[]{:S(2)}) collective-permute-start(f32[2,256,256]{2,1,0:T(8,128)} %get-tuple-element.341), channel_id=1, source_target_pairs={{0,2},{2,0},{1,3},{3,1},{4,6},{6,4},{5,7},{7,5},{8,10},{10,8},{9,1... | collective-permute-start | bytes 1572872 | tf_op jit(solution)/shard_map/ppermute | solution.py:358
  52.7 26.8 %copy-start.8 = (s32[8]{0:T(128)S(1)}, s32[8]{0:T(128)}, u32[]{:S(2)}) copy-start(s32[8]{0:T(128)} %pick_ref.3) | copy-start | bytes 100
  54.5 10.1 %collective-permute-start.5 = (f32[2,256,256]{2,1,0:T(8,128)S(1)}, f32[2,256,256]{2,1,0:T(8,128)S(1)}, u32[]{:S(2)}, u32[]{:S(2)}) collective-permute-start(f32[2,256,256]{2,1,0:T(8,128)S(1)} %get-tuple-element.212), channel_id=1, source_target_pairs={{0,4},{8,12},{4,0},{12,8},{1,5},{9,13},{5,1},{13,9},{2,6},{10,14},... | collective-permute-start | bytes 1572872 | tf_op jit(solution)/shard_map/cond/branch_1_fun/ppermute | solution.py:411
  57.3 7.2 %collective-permute-start.6 = (f32[2,256,256]{2,1,0:T(8,128)S(1)}, f32[2,256,256]{2,1,0:T(8,128)S(1)}, u32[]{:S(2)}, u32[]{:S(2)}) collective-permute-start(f32[2,256,256]{2,1,0:T(8,128)S(1)} %get-tuple-element.213), channel_id=1, source_target_pairs={{4,8},{8,4},{5,9},{9,5},{6,10},{10,6},{7,11},{11,7},{20,24},{24,20... | collective-permute-start | bytes 1572872 | tf_op jit(solution)/shard_map/cond/branch_1_fun/ppermute | solution.py:411
  58.2 9.2 %collective-permute-start.7 = (f32[2,256,256]{2,1,0:T(8,128)S(1)}, f32[2,256,256]{2,1,0:T(8,128)S(1)}, u32[]{:S(2)}, u32[]{:S(2)}) collective-permute-start(f32[2,256,256]{2,1,0:T(8,128)S(1)} %get-tuple-element.214), channel_id=1, source_target_pairs={{0,2},{2,0},{1,3},{3,1},{4,6},{6,4},{5,7},{7,5},{8,10},{10,8},{9,1... | collective-permute-start | bytes 1572872 | tf_op jit(solution)/shard_map/cond/branch_1_fun/ppermute | solution.py:358
  59.8 8.2 %collective-permute-start.4 = (f32[2,2,256,256]{3,2,1,0:T(8,128)S(1)}, f32[2,2,256,256]{3,2,1,0:T(8,128)S(1)}, u32[]{:S(2)}, u32[]{:S(2)}) collective-permute-start(f32[2,2,256,256]{3,2,1,0:T(8,128)S(1)} %get-tuple-element.202.refs_2_), channel_id=1, source_target_pairs={{0,1},{1,0},{2,3},{3,2},{4,5},{5,4},{6,7},{7,6},{8,9},{9,8},{10,11... | collective-permute-start | bytes 3145736 | tf_op jit(solution)/shard_map/cond/branch_1_fun/ppermute | solution.py:358
  59.8 8.2 %collective-permute-start.8 = (f32[2,256,256]{2,1,0:T(8,128)}, f32[2,256,256]{2,1,0:T(8,128)S(1)}, u32[]{:S(2)}, u32[]{:S(2)}) collective-permute-start(f32[2,256,256]{2,1,0:T(8,128)} %get-tuple-element.203.refs_6_.refs_4_), channel_id=1, source_target_pairs={{0,1},{1,0},{2,3},{3,2},{4,5},{5,4},{6,7},{7,6},{8,9},{9,8},{10,11... | collective-permute-start | bytes 1572872 | tf_op jit(solution)/shard_map/cond/branch_1_fun/ppermute | solution.py:358
  64.6 3.4 %collective-permute-start.9 = (f32[2,256,256]{2,1,0:T(8,128)}, f32[2,256,256]{2,1,0:T(8,128)S(1)}, u32[]{:S(2)}, u32[]{:S(2)}) collective-permute-start(f32[2,256,256]{2,1,0:T(8,128)} %get-tuple-element.204.refs_7_.refs_5_), channel_id=1, source_target_pairs={{0,1},{1,0},{2,3},{3,2},{4,5},{5,4},{6,7},{7,6},{8,9},{9,8},{10,11... | collective-permute-start | bytes 1572872 | tf_op jit(solution)/shard_map/cond/branch_1_fun/ppermute | solution.py:358
  67.5 1.9 %collective-permute-start.10 = (f32[2,256,256]{2,1,0:T(8,128)S(1)}, f32[2,256,256]{2,1,0:T(8,128)S(1)}, u32[]{:S(2)}, u32[]{:S(2)}) collective-permute-start(f32[2,256,256]{2,1,0:T(8,128)S(1)} %collective-permute-done.5.refs_6_), channel_id=1, source_target_pairs={{0,1},{1,0},{2,3},{3,2},{4,5},{5,4},{6,7},{7,6},{8,9},{9,8},{10,11... | collective-permute-start | bytes 1572872 | tf_op jit(solution)/shard_map/cond/branch_1_fun/ppermute | solution.py:358
  67.5 2.7 %collective-permute-start.11 = (f32[2,256,256]{2,1,0:T(8,128)S(1)}, f32[2,256,256]{2,1,0:T(8,128)S(1)}, u32[]{:S(2)}, u32[]{:S(2)}) collective-permute-start(f32[2,256,256]{2,1,0:T(8,128)S(1)} %collective-permute-done.6.refs_7_), channel_id=1, source_target_pairs={{0,1},{1,0},{2,3},{3,2},{4,5},{5,4},{6,7},{7,6},{8,9},{9,8},{10,11... | collective-permute-start | bytes 1572872 | tf_op jit(solution)/shard_map/cond/branch_1_fun/ppermute | solution.py:358
  79.3 3.1 %collective-permute-start.39 = (f32[2,2,256,256]{3,2,1,0:T(8,128)}, f32[2,2,256,256]{3,2,1,0:T(8,128)S(1)}, u32[]{:S(2)}, u32[]{:S(2)}) collective-permute-start(f32[2,2,256,256]{3,2,1,0:T(8,128)} %get-tuple-element.687.s_ref), channel_id=1, source_target_pairs={{0,1},{1,0},{2,3},{3,2},{4,5},{5,4},{6,7},{7,6},{8,9},{9,8},{10,11... | collective-permute-start | bytes 3145736 | tf_op jit(solution)/shard_map/ppermute | solution.py:358
  (5 other events, 54.2 us)
